TPU v7x, 32 devices: a whole 2x2x4 slice. The times are simulated.
32 devices in a mesh: groups: 2 (over y), enc: 4 (over z), dec: 2 (over x), mp: 2 (over core).
Axes of the slice: x: 2, y: 2, z: 4, core: 2. Of those that a mesh axis runs over, the one named last changes fastest.
Arguments:
- tokens: bfloat16 [4, 16, 16, 16, 1280], P(('groups', 'dec'), 'enc'), parts along dimension 0, may hold values from -6 to 6
- gain_pre: float32 [1280], replicated, may hold values from 0.5 to 2
- w_up: bfloat16 [1280, 2560], P('enc', 'mp'), may hold values from -0.15625 to 0.15625
- w_down: bfloat16 [2560, 1280], P('mp', 'enc'), may hold values from -0.125 to 0.125
- gain_post: float32 [1280], replicated, may hold values from 0.5 to 2
- w_neck: bfloat16 [1280, 256], replicated, may hold values from -0.15625 to 0.15625
- conv_weight: bfloat16 [3, 3, 256, 256], P(None, None, None, 'mp'), may hold values from -0.125 to 0.125
- conv_bias: float32 [256], P('mp'), may hold values from -3 to 3
- cls_weight: bfloat16 [256, 13], P('mp'), may hold values from -0.375 to 0.375
- cls_bias: float32 [13], replicated, may hold values from -4 to 4
- tile_table: int32 [4, 16, 2], P(('groups', 'dec')), parts along dimension 0, may hold values from -1 to 16, as said below
- labels: int32 [8, 4, 96], P(None, 'enc', ('groups', 'dec')), parts along dimension 2, may hold values from 0 to 12
Outputs:
- logits: float32 [8, 4, 96, 13], P(None, 'enc', ('groups', 'dec')), parts along dimension 2
- nll: float32 [8, 4, 96], P(None, 'enc', ('groups', 'dec')), parts along dimension 2
There are 2 independent parts, one for each index of `groups`. A program takes and returns all parts, laid end to end along the dimension named above; an argument that names none is the same for every part. Nothing has to cross between parts.
Inputs may be any that keep to these rules, and one draw needn't show every extreme that they name: `tile_table`: in every band each tile corner with strip row a multiple of 8 from 0 to 16 and band column 0 or 8 stands in exactly one slot; all other slots are empty; in every band one encoder rank holds 4 tiles.
All inputs are finite; a program needn't handle non-finite values.
Results may differ from a plain program's by a relative error of at most 0.0075.
Values may be sent and summed in bfloat16 or wider, within the bound.
A program may use at most 64 MiB of HBM per device.

v0:
```python
import functools

import jax
import jax.numpy as jnp
from jax import lax
from jax.experimental import pallas as pl
from jax.experimental.pallas import tpu as pltpu
from jax.sharding import PartitionSpec as P

TS = 16


norm_eps = 1e-05
blend_sigma = 4.0


def layer_norm(values, scale_vec):
    row_mean = jnp.mean(values, axis=-1, keepdims=True)
    centered = values - row_mean
    row_var = jnp.mean(centered * centered, axis=-1, keepdims=True)
    return centered * lax.rsqrt(row_var + norm_eps) * scale_vec


MESH = pl.DeviceIdType.MESH
COLS = 256


def strip_kernel(
    sizes, sizes_rows, tok, gain_pre, w_up, w_down_t, gain_post, w_neck, conv_hbm, conv_bias, cls_t, table,
    cls_bias, labels, out, out_nll,
    gains, weights, xs, normed, hidden, give, take, own, neck,
    conv_w, deal, dealt, spread, denom, part_sum, other_sum, merged, halo, edge, edges_in,
    part_logits, other_logits,
    local_sem, recv_sem, send_sem, give_sem, take_sem,
    deal_send, deal_recv, pair_send, pair_recv, halo_send, halo_recv, edge_send, edge_recv,
):
    groups, enc, dec = sizes
    y, z = lax.axis_index("groups"), lax.axis_index("enc")
    x, m = lax.axis_index("dec"), lax.axis_index("mp")
    blk, ff = w_up.shape
    total, width = xs.shape
    spread_rows = sizes_rows
    half = total // 2
    split = groups % 2 == 0 and dec % 2 == 0 and blk % 64 == 0
    parts = 4 if split else 1
    piece = blk // parts
    ox, oy = x + 1 - 2 * (x % 2), y + 1 - 2 * (y % 2)
    mine = (y % 2) * 2 + x % 2 if split else 0
    of_x = (y % 2) * 2 + 1 - x % 2
    of_y = (1 - y % 2) * 2 + x % 2
    diagonal = (1 - y % 2) * 2 + 1 - x % 2

    def region(mat, block, quarter):
        start = pl.multiple_of(block * blk + quarter * piece, 16)
        return weights.at[mat, pl.ds(start, piece)]

    def copy(mat, block, quarter, kind, target, sent, own_src=False):
        dst = region(mat, block, quarter)
        src = dst
        if own_src:
            start = pl.multiple_of(quarter * piece, 16)
            src = (w_up, w_down_t)[mat].at[pl.ds(start, piece)]
        return pltpu.make_async_remote_copy(
            src_ref=src, dst_ref=dst,
            send_sem=send_sem.at[mat, block, sent], recv_sem=recv_sem.at[mat, block, kind],
            device_id=target, device_id_type=MESH,
        )

    up_z, down_z = {"enc": z + 1}, {"enc": z - 1}
    to_x, to_y = {"dec": ox}, {"groups": oy}

    def own_sends(mat):
        right = copy(mat, z, mine, 0, up_z, 0, True)
        left = copy(mat, z, mine, 0, down_z, 1, True)
        if not split:
            return (right,), (left,)
        right_diagonal = copy(mat, z, diagonal, 3, up_z, 4, True)
        left_diagonal = copy(mat, z, diagonal, 3, down_z, 5, True)
        return (right, right_diagonal), (left, left_diagonal)

    def start_own(mat, first, last):
        right, left = own_sends(mat)
        right, left = right[first:last], left[first:last]

        @pl.when(z < enc - 1)
        def _():
            for item in right:
                item.start()

        @pl.when(z > 0)
        def _():
            for item in left:
                item.start()

    def z_step(mat, far):
        @pl.when(z - far >= 0)
        def _():
            block = z - far
            copy(mat, block, mine, 0, up_z, 0).wait_recv()

            @pl.when(z < enc - 1)
            def _():
                copy(mat, block, mine, 0, up_z, 0).start()

            if split:
                copy(mat, block, mine, 1, to_x, 2).start()
                copy(mat, block, mine, 2, to_y, 3).start()

        @pl.when(z + far < enc)
        def _():
            block = z + far
            copy(mat, block, mine, 0, down_z, 1).wait_recv()

            @pl.when(z > 0)
            def _():
                copy(mat, block, mine, 0, down_z, 1).start()

            if split:
                copy(mat, block, mine, 1, to_x, 2).start()
                copy(mat, block, mine, 2, to_y, 3).start()

    def each_block(far, fn):
        @pl.when(z - far >= 0)
        def _():
            fn(z - far)

        @pl.when(z + far < enc)
        def _():
            fn(z + far)

    def plane_step(mat, far):
        if not split:
            return

        def one(block):
            by_y = (block + mat) % 2 == 0
            copy(mat, block, of_x, 1, to_x, 2).wait_recv()

            if far > 1:
                @pl.when(by_y)
                def _():
                    copy(mat, block, of_x, 3, to_y, 4).start()

            copy(mat, block, of_y, 2, to_y, 3).wait_recv()

            if far > 1:
                @pl.when(jnp.logical_not(by_y))
                def _():
                    copy(mat, block, of_y, 3, to_x, 4).start()

        each_block(far, one)

    def diagonal_step(mat, far):
        if split:
            each_block(far, lambda block: copy(mat, block, diagonal, 3, to_x, 4).wait_recv())

    def finish_sends(mat):
        right, left = own_sends(mat)

        @pl.when(z < enc - 1)
        def _():
            for item in right:
                item.wait_send()

        @pl.when(z > 0)
        def _():
            for item in left:
                item.wait_send()

        for far in range(1, enc):
            @pl.when((z - far >= 0) & (z < enc - 1))
            def _(far=far):
                copy(mat, z - far, mine, 0, up_z, 0).wait_send()

            @pl.when((z + far < enc) & (z > 0))
            def _(far=far):
                copy(mat, z + far, mine, 0, down_z, 1).wait_send()

            if split:
                def one(block, far=far):
                    copy(mat, block, mine, 1, to_x, 2).wait_send()
                    copy(mat, block, mine, 2, to_y, 3).wait_send()
                    if far > 1:
                        copy(mat, block, of_x, 3, to_x, 4).wait_send()

                each_block(far, one)

    start_of = pl.multiple_of(z * blk, 16)
    local = [
        pltpu.make_async_copy(tok, xs, local_sem.at[0]),
        pltpu.make_async_copy(w_up, weights.at[0, pl.ds(start_of, blk)], local_sem.at[1]),
        pltpu.make_async_copy(w_down_t, weights.at[1, pl.ds(start_of, blk)], local_sem.at[2]),
        pltpu.make_async_copy(w_neck, neck, local_sem.at[3]),
        pltpu.make_async_copy(conv_hbm, conv_w, local_sem.at[4]),
    ]
    for item in local:
        item.start()

    edges_in[...] = jnp.zeros_like(edges_in)
    above_z, below_z = (z + enc - 1) % enc, (z + 1) % enc
    barrier = pltpu.get_barrier_semaphore()

    def greet(**target):
        pl.semaphore_signal(barrier, inc=1, device_id=target, device_id_type=MESH)

    for off in range(1, enc):
        greet(enc=(z + off) % enc)
    greet(mp=1 - m)
    if split:
        greet(groups=oy)

    def greet_side(side_x):
        greet(dec=side_x)
        greet(dec=side_x, enc=above_z)
        greet(dec=side_x, enc=below_z)

    @pl.when(x > 0)
    def _():
        greet_side(x - 1)

    @pl.when(x < dec - 1)
    def _():
        greet_side(x + 1)

    sides = (x + dec - 1) // dec + 1 - (x + 1) // dec
    pl.semaphore_wait(barrier, enc + (1 if split else 0) + 3 * sides)

    start_own(0, 0, 1)
    local[0].wait()
    rows = 32

    def wide(ref):
        return jnp.concatenate([ref[i : i + 1, :] for i in range(ref.shape[0])], axis=1)

    gains[0:1, :] = wide(gain_pre)
    gains[1:2, :] = wide(gain_post)

    def first_norm(i, carry):
        at = pl.ds(pl.multiple_of(i * rows, rows), rows)
        normed[at, :] = layer_norm(xs[at, :].astype(jnp.float32), gains[0:1, :]).astype(jnp.bfloat16)
        return carry

    norm_steps = total // rows
    lax.fori_loop(0, norm_steps // 2, first_norm, 0)
    z_step(0, 1)
    lax.fori_loop(norm_steps // 2, norm_steps, first_norm, 0)
    for far in range(2, enc - 1):
        z_step(0, far)
    start_own(0, 1, 2)
    start_own(1, 0, 1)

    side = TS
    slots = total // (side * side)
    part = slots // 2
    row_groups = side // enc
    run = row_groups * side
    band = denom.shape[0] // spread_rows
    places = spread_rows * band
    lanes = enc * part * run
    lane = lax.broadcasted_iota(jnp.int32, (1, lanes), 1)
    strip_row = lax.broadcasted_iota(jnp.int32, (spread_rows, band, lanes), 0) * enc + z
    strip_row = strip_row.reshape(places, lanes)
    band_col = lax.broadcasted_iota(jnp.int32, (spread_rows, band, lanes), 1).reshape(places, lanes)

    def spread_of(owner):
        top = jnp.zeros((1, lanes), jnp.int32)
        left = jnp.zeros((1, lanes), jnp.int32)
        group = jnp.zeros((1, lanes), jnp.int32)
        col = lane
        for unit in range(enc * part):
            entry = (unit // part) * slots + owner * part + unit % part
            inside = lane >= unit * run
            top = jnp.where(inside, table[0, 0, entry], top)
            left = jnp.where(inside, table[0, 1, entry], left)
            for g in range(row_groups):
                begin = lane >= unit * run + g * side
                group = jnp.where(begin, g, group)
                col = jnp.where(begin, lane - (unit * run + g * side), col)
        tile_row = jnp.bitwise_and(group * enc + z - top, side - 1)
        middle = (side - 1) / 2.0
        dr = tile_row.astype(jnp.float32) - middle
        dc = col.astype(jnp.float32) - middle
        weight = jnp.exp(-(dr * dr + dc * dc) / (2.0 * blend_sigma * blend_sigma))
        weight = weight.astype(jnp.bfloat16).astype(jnp.float32)
        weight = jnp.where(top >= 0, weight, 0.0)
        hit = (strip_row == top + tile_row) & (band_col == left + col)
        return jnp.where(hit, weight, 0.0)

    mine_spread = spread_of(m)
    spread[...] = mine_spread.astype(jnp.bfloat16)
    denom[...] = jnp.sum(mine_spread + spread_of(1 - m), axis=1, keepdims=True)

    far_all = range(1, enc)
    if enc > 2:
        z_step(0, enc - 1)
    for far in range(2, enc):
        plane_step(0, far)
    z_step(1, 1)
    plane_step(0, 1)
    for far in far_all:
        diagonal_step(0, far)
    local[1].wait()

    col_steps = ff // COLS
    units = col_steps * 2

    def up_unit(i, carry):
        at = pl.ds(pl.multiple_of((i % 2) * half, half), half)
        cols = pl.ds(pl.multiple_of((i // 2) * COLS, COLS), COLS)
        value = jnp.dot(normed[at, :], weights[0, :, cols], preferred_element_type=jnp.float32)
        value = 0.5 * value * (1.0 + lax.erf(value * 0.7071067811865476))
        hidden[at, cols] = value.astype(jnp.bfloat16)
        return carry

    edges = [0, units // 5, units // 2, units * 7 // 10, units]
    lax.fori_loop(edges[0], edges[1], up_unit, 0)
    for far in range(2, enc - 1):
        z_step(1, far)
    start_own(1, 1, 2)
    lax.fori_loop(edges[1], edges[2], up_unit, 0)
    if enc > 2:
        z_step(1, enc - 1)
    for far in range(2, enc - 1):
        plane_step(1, far)
    lax.fori_loop(edges[2], edges[3], up_unit, 0)
    if enc > 2:
        plane_step(1, enc - 1)
    lax.fori_loop(edges[3], edges[4], up_unit, 0)
    plane_step(1, 1)
    for far in far_all:
        diagonal_step(1, far)
    local[2].wait()

    def down(first, dest, i):
        at = pl.ds(pl.multiple_of(first, half), half)
        cols = pl.ds(pl.multiple_of(i * COLS, COLS), COLS)
        value = lax.dot_general(
            hidden[at, :], weights[1, cols, :], (((1,), (1,)), ((), ())),
            preferred_element_type=jnp.float32,
        )
        dest[:, cols] = value.astype(jnp.bfloat16)

    def exchange(i):
        cols = pl.ds(pl.multiple_of(i * COLS, COLS), COLS)
        return pltpu.make_async_remote_copy(
            src_ref=give.at[:, cols], dst_ref=take.at[:, cols],
            send_sem=give_sem.at[i], recv_sem=take_sem.at[i],
            device_id={"mp": 1 - m}, device_id_type=MESH,
        )

    def other_half(i, carry):
        down((1 - m) * half, give, i)
        exchange(i).start()
        return carry

    def own_half(i, carry):
        down(m * half, own, i)
        return carry

    steps = width // COLS
    lax.fori_loop(0, steps, other_half, 0)
    lax.fori_loop(0, steps, own_half, 0)
    for i in range(steps):
        exchange(i).wait_recv()

    def second_norm(i, carry):
        at = pl.ds(pl.multiple_of(i * rows, rows), rows)
        whole = pl.ds(pl.multiple_of(m * half + i * rows, rows), rows)
        mixed = own[at, :].astype(jnp.float32) + take[at, :].astype(jnp.float32)
        value = xs[whole, :].astype(jnp.float32) + mixed
        normed[at, :] = layer_norm(value, gains[1:2, :]).astype(jnp.bfloat16)
        return carry

    lax.fori_loop(0, half // rows, second_norm, 0)
    local[3].wait()
    values = jnp.dot(
        normed[0:half, :], neck[...], preferred_element_type=jnp.float32
    ).astype(jnp.bfloat16)
    tile_size = side * side
    for slot in range(part):
        value = values[slot * tile_size : (slot + 1) * tile_size]
        top = table[0, 0, z * slots + m * part + slot]
        swapped = jnp.concatenate([value[tile_size // 2 :], value[: tile_size // 2]], axis=0)
        flag = jnp.bitwise_and(jnp.maximum(top, 0), side - 1) == side // 2
        value = jnp.where(flag, swapped.astype(jnp.float32), value.astype(jnp.float32)).astype(jnp.bfloat16)
        for row in range(side):
            at = slot * run + (row // enc) * side
            deal[row % enc, at : at + side, :] = value[row * side : (row + 1) * side]

    def deal_copy(off):
        target = (z + off) % enc
        return pltpu.make_async_remote_copy(
            src_ref=deal.at[target], dst_ref=dealt.at[z],
            send_sem=deal_send.at[off], recv_sem=deal_recv.at[off],
            device_id={"enc": target}, device_id_type=MESH,
        )

    for off in range(1, enc):
        deal_copy(off).start()
    dealt[z] = deal[z]
    local[4].wait()
    for off in range(1, enc):
        deal_copy(off).wait_recv()
    channels = deal.shape[2]
    numer = jnp.dot(
        spread[...], dealt[...].reshape(lanes, channels), preferred_element_type=jnp.float32
    )
    part_sum[...] = numer.astype(jnp.bfloat16)

    def pair(src, dst, which):
        return pltpu.make_async_remote_copy(
            src_ref=src, dst_ref=dst, send_sem=pair_send.at[which], recv_sem=pair_recv.at[which],
            device_id={"mp": 1 - m}, device_id_type=MESH,
        )

    swap_sum = pair(part_sum, other_sum, 0)
    swap_sum.start()
    swap_sum.wait_recv()
    numer = part_sum[...].astype(jnp.float32) + other_sum[...].astype(jnp.float32)
    whole = numer / denom[...]
    merged[...] = whole.astype(jnp.bfloat16)

    def halo_copy(which):
        return pltpu.make_async_remote_copy(
            src_ref=merged, dst_ref=halo.at[which],
            send_sem=halo_send.at[which], recv_sem=halo_recv.at[which],
            device_id={"enc": (below_z, above_z)[which]}, device_id_type=MESH,
        )

    halo_copy(0).start()
    halo_copy(1).start()
    cube = whole.reshape(spread_rows, band, channels)
    blank = jnp.zeros((edge.shape[1] - spread_rows, channels), jnp.float32)
    edge[0] = jnp.concatenate([cube[:, 0, :], blank], axis=0).astype(jnp.bfloat16)
    edge[1] = jnp.concatenate([cube[:, band - 1, :], blank], axis=0).astype(jnp.bfloat16)

    def edge_copy(which, level):
        target = {"dec": (x - 1, x + 1)[which]}
        if level:
            target["enc"] = (below_z, above_z)[level - 1]
        return pltpu.make_async_remote_copy(
            src_ref=edge.at[which], dst_ref=edges_in.at[1 - which, level],
            send_sem=edge_send.at[which, level], recv_sem=edge_recv.at[1 - which, level],
            device_id=target, device_id_type=MESH,
        )

    def every_edge(which, act):
        @pl.when((x > 0) if which == 0 else (x < dec - 1))
        def _():
            for level in range(3):
                act(edge_copy(which, level))

    every_edge(0, lambda c: c.start())
    every_edge(1, lambda c: c.start())

    kinds = conv_w.shape[3]

    def products(source, row_off):
        return [
            jnp.dot(source, conv_w[row_off, b], preferred_element_type=jnp.float32) for b in range(3)
        ]

    spot = lax.broadcasted_iota(jnp.int32, (spread_rows, band, kinds), 0).reshape(places, kinds)
    spot_col = lax.broadcasted_iota(jnp.int32, (spread_rows, band, kinds), 1).reshape(places, kinds)
    center = products(merged[...], 1)

    def moved_down(value, step, index):
        shifted_value = jnp.where(index == 0, 0.0, pltpu.roll(value, step, 0))
        return jnp.where(z == 0, shifted_value, value)

    def moved_up(value, step, index):
        size = value.shape[0]
        shifted_value = jnp.where(index == spread_rows - 1, 0.0, pltpu.roll(value, size - step, 0))
        return jnp.where(z == enc - 1, shifted_value, value)

    halo_copy(0).wait_recv()
    upper = products(halo[0], 0)
    halo_copy(1).wait_recv()
    lower = products(halo[1], 2)
    for which in range(2):
        every_edge(1 - which, lambda c: c.wait_send())

    @pl.when(x < dec - 1)
    def _():
        for level in range(3):
            edge_copy(0, level).wait_recv()

    @pl.when(x > 0)
    def _():
        for level in range(3):
            edge_copy(1, level).wait_recv()

    sums = [
        center[b] + moved_down(upper[b], band, spot) + moved_up(lower[b], band, spot) for b in range(3)
    ]
    index = lax.broadcasted_iota(jnp.int32, (edge.shape[1], kinds), 0)

    def edge_sum(which, b):
        levels = [
            jnp.dot(edges_in[which, level], conv_w[a, b], preferred_element_type=jnp.float32)
            for level, a in ((0, 1), (1, 0), (2, 2))
        ]
        value = levels[0] + moved_down(levels[1], 1, index) + moved_up(levels[2], 1, index)
        value = value[:spread_rows].reshape(spread_rows, 1, kinds)
        return jnp.broadcast_to(value, (spread_rows, band, kinds)).reshape(places, kinds)

    before = jnp.where(spot_col == 0, edge_sum(0, 0), pltpu.roll(sums[0], 1, 0))
    after = jnp.where(spot_col == band - 1, edge_sum(1, 2), pltpu.roll(sums[2], places - 1, 0))
    activ = jnp.maximum(sums[1] + before + after + conv_bias[...], 0.0).astype(jnp.bfloat16)
    part_logits[...] = lax.dot_general(
        cls_t[...], activ, (((1,), (1,)), ((), ())), preferred_element_type=jnp.float32
    )
    swap_logits = pair(part_logits, other_logits, 1)
    swap_logits.start()
    swap_logits.wait_recv()
    classes = out.shape[1]
    square = (classes, classes)
    same = lax.broadcasted_iota(jnp.int32, square, 0) == lax.broadcasted_iota(jnp.int32, square, 1)
    bias = jnp.sum(jnp.where(same, cls_bias[...], 0.0), axis=1, keepdims=True)
    logits = part_logits[...] + other_logits[...] + bias
    wanted = jnp.concatenate([labels[k] for k in range(spread_rows)], axis=1)
    ids = lax.broadcasted_iota(jnp.int32, (classes, places), 0)
    picked = jnp.sum(jnp.where(ids == wanted, logits, 0.0), axis=0, keepdims=True)
    nll = jnp.log(jnp.sum(jnp.exp(logits), axis=0, keepdims=True)) - picked
    for k in range(spread_rows):
        out_nll[k] = nll[:, k * band : (k + 1) * band]
        out[k] = logits[:, k * band : (k + 1) * band].reshape(classes, 1, band)

    swap_sum.wait_send()
    swap_logits.wait_send()
    halo_copy(0).wait_send()
    halo_copy(1).wait_send()
    for off in range(1, enc):
        deal_copy(off).wait_send()
    finish_sends(0)
    finish_sends(1)
    for i in range(steps):
        exchange(i).wait_send()


def body(
    tokens,
    gain_pre,
    w_up,
    w_down,
    gain_post,
    w_neck,
    conv_weight,
    conv_bias,
    cls_weight,
    cls_bias,
    tile_table,
    labels,
):
    sizes = tuple(lax.axis_size(name) for name in ("groups", "enc", "dec"))
    enc = sizes[1]
    blk, ff = w_up.shape
    width = tokens.shape[-1]
    flat = tokens.reshape(-1, width)
    total = flat.shape[0]
    half = total // 2
    rows_local, _, band = labels.shape
    places = rows_local * band
    channels = w_neck.shape[1]
    classes = cls_weight.shape[1]
    dealt_rows = half // enc
    edge_rows = -(-rows_local // 16) * 16
    bf16, f32 = jnp.bfloat16, jnp.float32
    vmem = pl.BlockSpec(memory_space=pltpu.VMEM)
    anywhere = pl.BlockSpec(memory_space=pl.ANY)
    dma = pltpu.SemaphoreType.DMA
    logits, nll = pl.pallas_call(
        functools.partial(strip_kernel, sizes, rows_local),
        out_shape=(
            jax.ShapeDtypeStruct((rows_local, classes, 1, band), f32),
            jax.ShapeDtypeStruct(labels.shape, f32),
        ),
        in_specs=[anywhere, vmem, anywhere, anywhere, vmem, anywhere, anywhere, vmem, vmem,
                  pl.BlockSpec(memory_space=pltpu.SMEM), vmem, vmem],
        out_specs=(vmem, vmem),
        scratch_shapes=[
            pltpu.VMEM((2, width), f32),
            pltpu.VMEM((2, width, ff), bf16),
            pltpu.VMEM((total, width), bf16),
            pltpu.VMEM((total, width), bf16),
            pltpu.VMEM((total, ff), bf16),
            pltpu.VMEM((half, width), bf16),
            pltpu.VMEM((half, width), bf16),
            pltpu.VMEM((half, width), bf16),
            pltpu.VMEM(w_neck.shape, bf16),
            pltpu.VMEM(conv_weight.shape, bf16),
            pltpu.VMEM((enc, dealt_rows, channels), bf16),
            pltpu.VMEM((enc, dealt_rows, channels), bf16),
            pltpu.VMEM((places, half), bf16),
            pltpu.VMEM((places, 1), f32),
            pltpu.VMEM((places, channels), bf16),
            pltpu.VMEM((places, channels), bf16),
            pltpu.VMEM((places, channels), bf16),
            pltpu.VMEM((2, places, channels), bf16),
            pltpu.VMEM((2, edge_rows, channels), bf16),
            pltpu.VMEM((2, 3, edge_rows, channels), bf16),
            pltpu.VMEM((classes, places), f32),
            pltpu.VMEM((classes, places), f32),
            dma((5,)),
            dma((2, enc, 4)),
            dma((2, enc, 6)),
            dma((width // COLS,)),
            dma((width // COLS,)),
            dma((enc,)),
            dma((enc,)),
            dma((2,)),
            dma((2,)),
            dma((2,)),
            dma((2,)),
            dma((2, 3)),
            dma((2, 3)),
        ],
        compiler_params=pltpu.CompilerParams(
            collective_id=0, has_side_effects=True, vmem_limit_bytes=60 * 1024 * 1024
        ),
    )(
        flat, gain_pre.reshape(-1, 128), w_up, w_down.T, gain_post.reshape(-1, 128), w_neck,
        conv_weight, conv_bias.reshape(1, -1), cls_weight.T, jnp.swapaxes(tile_table, 1, 2),
        cls_bias.reshape(1, -1), labels,
    )
    logits = jnp.transpose(logits, (0, 2, 3, 1))
    return (logits, nll)


def solution(mesh):
    in_specs = (
        P(("groups", "dec"), "enc", None, None, None),
        P(),
        P("enc", "mp"),
        P("mp", "enc"),
        P(),
        P(),
        P(None, None, None, "mp"),
        P("mp"),
        P("mp", None),
        P(),
        P(("groups", "dec"), None, None),
        P(None, "enc", ("groups", "dec")),
    )
    out_specs = (P(None, "enc", ("groups", "dec"), None), P(None, "enc", ("groups", "dec")))
    return jax.shard_map(body, mesh=mesh, in_specs=in_specs, out_specs=out_specs, check_vma=False)
```

profile of v0, /device:TPU:0, one launch (start us, length us, event | category | flops | bytes accessed | tf_op | source)
XLA Modules:
  0.0 85.5 jit_solution(16776382661167064419)
XLA Ops:
  0.6 82.2 %shard_map.131 = (f32[8,13,1,24]{3,2,1,0:T(1,128)}, f32[8,1,24]{2,1,0:T(1,128)}) custom-call(bf16[1024,1280]{1,0:T(8,128)(2,1)} %bitcast.9, f32[10,128]{1,0:T(8,128)} %bitcast.12, bf16[320,1280]{1,0:T(8,128)(2,1)} %w_up.1, bf16[320,1280]{1,0:T(8,128)(2,1)} %bitcast.10, f32[10,128]{1,0:T(8,128)} %bitcast.13, bf16[1280,256]{1,0:T(8,128)(2,1)} %w_neck.1, ...), custom_call_target="tpu_custom_call" | custom-call | tf_op jit(solution)/shard_map/pallas_call | solution.py:572
  82.8 1.4 %copy.16 = f32[8,1,24,13]{2,1,3,0:T(1,128)} copy(f32[8,1,24,13]{2,1,3,0:T(1,128)} %bitcast.11) | data formatting | bytes 19968
  84.3 1.3 %copy.17 = f32[8,1,24]{2,1,0:T(1,128)} copy(f32[8,1,24]{2,1,0:T(1,128)} %get-tuple-element.9) | data formatting | bytes 1536
where the time goes:
time: 85.8 us; the launch traced here: 85.5 us
  Pallas kernels  82.2 us (96%)
  local copies, waits for them, and re-layouts  2.71 us (3%)
    pallas_call x1, Pallas kernels, body(): pl.pallas_call(functools.partial(strip_kernel, sizes, rows_local), out_sh...  82.2 us
    unnamed x2, local copies, waits for them, and re-layouts  2.71 us

commit v1 on v0

--- a/solution.py
+++ b/solution.py
@@ -38,6 +38,7 @@
     y, z = lax.axis_index("groups"), lax.axis_index("enc")
     x, m = lax.axis_index("dec"), lax.axis_index("mp")
     blk, ff = w_up.shape
+    half_ff = ff // 2
     total, width = xs.shape
     spread_rows = sizes_rows
     half = total // 2
@@ -59,7 +60,9 @@
         src = dst
         if own_src:
             start = pl.multiple_of(quarter * piece, 16)
-            src = (w_up, w_down_t)[mat].at[pl.ds(start, piece)]
+            src = (w_up, w_down_t)[mat // 2].at[
+                pl.ds(start, piece), pl.ds((mat % 2) * half_ff, half_ff)
+            ]
         return pltpu.make_async_remote_copy(
             src_ref=src, dst_ref=dst,
             send_sem=send_sem.at[mat, block, sent], recv_sem=recv_sem.at[mat, block, kind],
@@ -188,10 +191,15 @@
     start_of = pl.multiple_of(z * blk, 16)
     local = [
         pltpu.make_async_copy(tok, xs, local_sem.at[0]),
-        pltpu.make_async_copy(w_up, weights.at[0, pl.ds(start_of, blk)], local_sem.at[1]),
-        pltpu.make_async_copy(w_down_t, weights.at[1, pl.ds(start_of, blk)], local_sem.at[2]),
         pltpu.make_async_copy(w_neck, neck, local_sem.at[3]),
         pltpu.make_async_copy(conv_hbm, conv_w, local_sem.at[4]),
+    ] + [
+        pltpu.make_async_copy(
+            (w_up, w_down_t)[mat // 2].at[:, pl.ds((mat % 2) * half_ff, half_ff)],
+            weights.at[mat, pl.ds(start_of, blk)],
+            local_sem.at[(1, 2, 5, 6)[mat]],
+        )
+        for mat in range(4)
     ]
     for item in local:
         item.start()
@@ -291,52 +299,64 @@
     denom[...] = jnp.sum(mine_spread + spread_of(1 - m), axis=1, keepdims=True)
 
     far_all = range(1, enc)
-    if enc > 2:
-        z_step(0, enc - 1)
-    for far in range(2, enc):
-        plane_step(0, far)
-    z_step(1, 1)
-    plane_step(0, 1)
-    for far in far_all:
-        diagonal_step(0, far)
-    local[1].wait()
-
-    col_steps = ff // COLS
-    units = col_steps * 2
-
-    def up_unit(i, carry):
-        at = pl.ds(pl.multiple_of((i % 2) * half, half), half)
-        cols = pl.ds(pl.multiple_of((i // 2) * COLS, COLS), COLS)
-        value = jnp.dot(normed[at, :], weights[0, :, cols], preferred_element_type=jnp.float32)
-        value = 0.5 * value * (1.0 + lax.erf(value * 0.7071067811865476))
-        hidden[at, cols] = value.astype(jnp.bfloat16)
-        return carry
-
-    edges = [0, units // 5, units // 2, units * 7 // 10, units]
-    lax.fori_loop(edges[0], edges[1], up_unit, 0)
-    for far in range(2, enc - 1):
-        z_step(1, far)
-    start_own(1, 1, 2)
-    lax.fori_loop(edges[1], edges[2], up_unit, 0)
-    if enc > 2:
-        z_step(1, enc - 1)
-    for far in range(2, enc - 1):
-        plane_step(1, far)
-    lax.fori_loop(edges[2], edges[3], up_unit, 0)
-    if enc > 2:
-        plane_step(1, enc - 1)
-    lax.fori_loop(edges[3], edges[4], up_unit, 0)
-    plane_step(1, 1)
-    for far in far_all:
-        diagonal_step(1, far)
-    local[2].wait()
+    row_chunk = total // 4
+
+    def up_unit(mat):
+        def unit(i, carry):
+            at = pl.ds(pl.multiple_of(i * row_chunk, row_chunk), row_chunk)
+            value = jnp.dot(normed[at, :], weights[mat], preferred_element_type=jnp.float32)
+            value = 0.5 * value * (1.0 + lax.erf(value * 0.7071067811865476))
+            hidden[at, mat * half_ff : (mat + 1) * half_ff] = value.astype(jnp.bfloat16)
+            return carry
+
+        return unit
+
+    def rest_of(mat):
+        if enc > 2:
+            z_step(mat, enc - 1)
+        for far in range(2, enc):
+            plane_step(mat, far)
+        if mat < 3:
+            z_step(mat + 1, 1)
+        plane_step(mat, 1)
+
+    def early_of(mat):
+        for far in range(2, enc - 1):
+            z_step(mat, far)
+        start_own(mat, 1, 2)
+        if mat < 3:
+            start_own(mat + 1, 0, 1)
+
+    def last_of(mat):
+        for far in far_all:
+            diagonal_step(mat, far)
+        local[3 + mat].wait()
+
+    rest_of(0)
+    early_of(1)
+    last_of(0)
+    lax.fori_loop(0, 2, up_unit(0), 0)
+    rest_of(1)
+    lax.fori_loop(2, 4, up_unit(0), 0)
+    early_of(2)
+    last_of(1)
+    lax.fori_loop(0, 2, up_unit(1), 0)
+    rest_of(2)
+    early_of(3)
+    lax.fori_loop(2, 4, up_unit(1), 0)
+    last_of(2)
+    rest_of(3)
+    last_of(3)
 
     def down(first, dest, i):
         at = pl.ds(pl.multiple_of(first, half), half)
         cols = pl.ds(pl.multiple_of(i * COLS, COLS), COLS)
-        value = lax.dot_general(
-            hidden[at, :], weights[1, cols, :], (((1,), (1,)), ((), ())),
-            preferred_element_type=jnp.float32,
+        value = sum(
+            lax.dot_general(
+                hidden[at, mat * half_ff : (mat + 1) * half_ff], weights[2 + mat, cols, :],
+                (((1,), (1,)), ((), ())), preferred_element_type=jnp.float32,
+            )
+            for mat in range(2)
         )
         dest[:, cols] = value.astype(jnp.bfloat16)
 
@@ -372,7 +392,7 @@
         return carry
 
     lax.fori_loop(0, half // rows, second_norm, 0)
-    local[3].wait()
+    local[1].wait()
     values = jnp.dot(
         normed[0:half, :], neck[...], preferred_element_type=jnp.float32
     ).astype(jnp.bfloat16)
@@ -398,7 +418,7 @@
     for off in range(1, enc):
         deal_copy(off).start()
     dealt[z] = deal[z]
-    local[4].wait()
+    local[2].wait()
     for off in range(1, enc):
         deal_copy(off).wait_recv()
     channels = deal.shape[2]
@@ -532,8 +552,8 @@
     halo_copy(1).wait_send()
     for off in range(1, enc):
         deal_copy(off).wait_send()
-    finish_sends(0)
-    finish_sends(1)
+    for mat in range(4):
+        finish_sends(mat)
     for i in range(steps):
         exchange(i).wait_send()
 
@@ -580,7 +600,7 @@
         out_specs=(vmem, vmem),
         scratch_shapes=[
             pltpu.VMEM((2, width), f32),
-            pltpu.VMEM((2, width, ff), bf16),
+            pltpu.VMEM((4, width, ff // 2), bf16),
             pltpu.VMEM((total, width), bf16),
             pltpu.VMEM((total, width), bf16),
             pltpu.VMEM((total, ff), bf16),
@@ -601,9 +621,9 @@
             pltpu.VMEM((2, 3, edge_rows, channels), bf16),
             pltpu.VMEM((classes, places), f32),
             pltpu.VMEM((classes, places), f32),
-            dma((5,)),
-            dma((2, enc, 4)),
-            dma((2, enc, 6)),
+            dma((7,)),
+            dma((4, enc, 4)),
+            dma((4, enc, 6)),
             dma((width // COLS,)),
             dma((width // COLS,)),
             dma((enc,)),

time: 85.8 us -> 88.7 us (1.034)
  Pallas kernels: 82.2 us -> 85.1 us
    pallas_call x1, Pallas kernels: 82.2 us -> 85.1 us  [body(): pl.pallas_call(functools.partial(strip_kernel, sizes, rows_local), out_sh...]
where the time goes in v1:
time: 88.7 us; the launch traced here: 88.5 us
  Pallas kernels  85.1 us (96%)
  local copies, waits for them, and re-layouts  2.71 us (3%)
    pallas_call x1, Pallas kernels, body(): pl.pallas_call(functools.partial(strip_kernel, sizes, rows_local), out_sh...  85.1 us
    unnamed x2, local copies, waits for them, and re-layouts  2.71 us

profile of v1, /device:TPU:0, one launch (start us, length us, event | category | flops | bytes accessed | tf_op | source)
XLA Modules:
  0.0 88.5 jit_solution(9015209366595149900)
XLA Ops:
  0.6 85.1 %shard_map.131 = (f32[8,13,1,24]{3,2,1,0:T(1,128)}, f32[8,1,24]{2,1,0:T(1,128)}) custom-call(bf16[1024,1280]{1,0:T(8,128)(2,1)} %bitcast.9, f32[10,128]{1,0:T(8,128)} %bitcast.12, bf16[320,1280]{1,0:T(8,128)(2,1)} %w_up.1, bf16[320,1280]{1,0:T(8,128)(2,1)} %bitcast.10, f32[10,128]{1,0:T(8,128)} %bitcast.13, bf16[1280,256]{1,0:T(8,128)(2,1)} %w_neck.1, ...), custom_call_target="tpu_custom_call" | custom-call | tf_op jit(solution)/shard_map/pallas_call | solution.py:592
  85.8 1.4 %copy.16 = f32[8,1,24,13]{2,1,3,0:T(1,128)} copy(f32[8,1,24,13]{2,1,3,0:T(1,128)} %bitcast.11) | data formatting | bytes 19968
  87.2 1.3 %copy.17 = f32[8,1,24]{2,1,0:T(1,128)} copy(f32[8,1,24]{2,1,0:T(1,128)} %get-tuple-element.9) | data formatting | bytes 1536

commit v2 on v0

--- a/solution.py
+++ b/solution.py
@@ -28,7 +28,7 @@
 def strip_kernel(
     sizes, sizes_rows, tok, gain_pre, w_up, w_down_t, gain_post, w_neck, conv_hbm, conv_bias, cls_t, table,
     cls_bias, labels, out, out_nll,
-    gains, weights, xs, normed, hidden, give, take, own, neck,
+    gains, weights, xs, normed, hidden, give, take, neck,
     conv_w, deal, dealt, spread, denom, part_sum, other_sum, merged, halo, edge, edges_in,
     part_logits, other_logits,
     local_sem, recv_sem, send_sem, give_sem, take_sem,
@@ -331,42 +331,34 @@
         diagonal_step(1, far)
     local[2].wait()
 
-    def down(first, dest, i):
-        at = pl.ds(pl.multiple_of(first, half), half)
-        cols = pl.ds(pl.multiple_of(i * COLS, COLS), COLS)
-        value = lax.dot_general(
-            hidden[at, :], weights[1, cols, :], (((1,), (1,)), ((), ())),
-            preferred_element_type=jnp.float32,
-        )
-        dest[:, cols] = value.astype(jnp.bfloat16)
-
     def exchange(i):
         cols = pl.ds(pl.multiple_of(i * COLS, COLS), COLS)
         return pltpu.make_async_remote_copy(
-            src_ref=give.at[:, cols], dst_ref=take.at[:, cols],
+            src_ref=give.at[1 - m, :, cols], dst_ref=take.at[:, cols],
             send_sem=give_sem.at[i], recv_sem=take_sem.at[i],
             device_id={"mp": 1 - m}, device_id_type=MESH,
         )
 
-    def other_half(i, carry):
-        down((1 - m) * half, give, i)
+    def down(i, carry):
+        cols = pl.ds(pl.multiple_of(i * COLS, COLS), COLS)
+        value = lax.dot_general(
+            hidden[...], weights[1, cols, :], (((1,), (1,)), ((), ())),
+            preferred_element_type=jnp.float32,
+        ).astype(jnp.bfloat16)
+        give[0, :, cols] = value[:half]
+        give[1, :, cols] = value[half:]
         exchange(i).start()
         return carry
 
-    def own_half(i, carry):
-        down(m * half, own, i)
-        return carry
-
     steps = width // COLS
-    lax.fori_loop(0, steps, other_half, 0)
-    lax.fori_loop(0, steps, own_half, 0)
+    lax.fori_loop(0, steps, down, 0)
     for i in range(steps):
         exchange(i).wait_recv()
 
     def second_norm(i, carry):
         at = pl.ds(pl.multiple_of(i * rows, rows), rows)
         whole = pl.ds(pl.multiple_of(m * half + i * rows, rows), rows)
-        mixed = own[at, :].astype(jnp.float32) + take[at, :].astype(jnp.float32)
+        mixed = give[m, at, :].astype(jnp.float32) + take[at, :].astype(jnp.float32)
         value = xs[whole, :].astype(jnp.float32) + mixed
         normed[at, :] = layer_norm(value, gains[1:2, :]).astype(jnp.bfloat16)
         return carry
@@ -584,8 +576,7 @@
             pltpu.VMEM((total, width), bf16),
             pltpu.VMEM((total, width), bf16),
             pltpu.VMEM((total, ff), bf16),
-            pltpu.VMEM((half, width), bf16),
-            pltpu.VMEM((half, width), bf16),
+            pltpu.VMEM((2, half, width), bf16),
             pltpu.VMEM((half, width), bf16),
             pltpu.VMEM(w_neck.shape, bf16),
             pltpu.VMEM(conv_weight.shape, bf16),

time: 85.8 us -> 86.7 us (1.010)
  no operation moved by 1% of the time
where the time goes in v2:
time: 86.7 us; the launch traced here: 86.2 us
  Pallas kernels  82.9 us (96%)
  local copies, waits for them, and re-layouts  2.71 us (3%)
    pallas_call x1, Pallas kernels, body(): pl.pallas_call(functools.partial(strip_kernel, sizes, rows_local), out_sh...  82.9 us
    unnamed x2, local copies, waits for them, and re-layouts  2.71 us

profile of v2, /device:TPU:0, one launch (start us, length us, event | category | flops | bytes accessed | tf_op | source)
XLA Modules:
  0.0 86.2 jit_solution(5507112495339490537)
XLA Ops:
  0.6 82.9 %shard_map.131 = (f32[8,13,1,24]{3,2,1,0:T(1,128)}, f32[8,1,24]{2,1,0:T(1,128)}) custom-call(bf16[1024,1280]{1,0:T(8,128)(2,1)} %bitcast.9, f32[10,128]{1,0:T(8,128)} %bitcast.12, bf16[320,1280]{1,0:T(8,128)(2,1)} %w_up.1, bf16[320,1280]{1,0:T(8,128)(2,1)} %bitcast.10, f32[10,128]{1,0:T(8,128)} %bitcast.13, bf16[1280,256]{1,0:T(8,128)(2,1)} %w_neck.1, ...), custom_call_target="tpu_custom_call" | custom-call | tf_op jit(solution)/shard_map/pallas_call | solution.py:564
  83.5 1.4 %copy.16 = f32[8,1,24,13]{2,1,3,0:T(1,128)} copy(f32[8,1,24,13]{2,1,3,0:T(1,128)} %bitcast.11) | data formatting | bytes 19968
  85.0 1.3 %copy.17 = f32[8,1,24]{2,1,0:T(1,128)} copy(f32[8,1,24]{2,1,0:T(1,128)} %get-tuple-element.9) | data formatting | bytes 1536
